TPU v7x, 32 devices: a whole 2x2x4 slice. The times are simulated.
32 devices in a mesh: leaf: 8 (over z, y), near: 4 (over x, core).
Axes of the slice: x: 2, y: 2, z: 4, core: 2. Of those that a mesh axis runs over, the one named last changes fastest.
Arguments:
- coords: bfloat16 [512, 3, 256], P(('leaf', 'near')), may hold values from 0 to 1
- vectors: float32 [512, 64, 256], P(('leaf', 'near')), may hold values from -6 to 6
- near_list: int32 [512, 16], P(('leaf', 'near')), may hold values from 0 to 511, as said below
- near_count: int32 [512], P(('leaf', 'near')), may hold values from 2 to 16, as said below
- basis_up: float32 [512, 64, 256], P(('leaf', 'near')), may hold values from -0.375 to 0.375
- basis_down: float32 [512, 64, 256], P(('leaf', 'near')), may hold values from -0.75 to 0.75
- up_leaf: float32 [512, 64, 64], P(('leaf', 'near')), may hold values from -0.25 to 0.25
- down_leaf: float32 [512, 64, 64], P(('leaf', 'near')), may hold values from -0.75 to 0.75
- skeleton_box: float32 [64, 3, 64], P(('leaf', 'near')), may hold values from 0 to 1
- far_box: int32 [64, 8], P(('leaf', 'near')), may hold values from 0 to 63, as said below
- up_box: float32 [64, 64, 64], P(('leaf', 'near')), may hold values from -0.5 to 0.5
- down_box: float32 [64, 64, 64], P(('leaf', 'near')), may hold values from -0.75 to 0.75
- skeleton_device: float32 [32, 3, 64], P(('leaf', 'near')), may hold values from 0 to 1
- far_device: int32 [32, 8], P(('leaf', 'near')), may hold values from 0 to 31, as said below
- up_device: float32 [32, 64, 64], P(('leaf', 'near')), may hold values from -0.375 to 0.375
- down_device: float32 [32, 64, 64], P(('leaf', 'near')), may hold values from -0.75 to 0.75
- skeleton_top: float32 [16, 3, 64], replicated, may hold values from 0 to 1
- up_top: float32 [16, 64, 64], replicated, may hold values from -0.5 to 0.5
- down_top: float32 [16, 64, 64], replicated, may hold values from -0.75 to 0.75
Outputs:
- product: float32 [512, 64, 256], P(('leaf', 'near'))
Inputs may be any that keep to these rules, and one draw needn't show every extreme that they name: `near_list`: slot 0 of each leaf's list names the leaf itself, and so does every slot at or beyond its count. Every entry names a leaf of a device with the same leaf index (devices are numbered leaf index times 4 plus near index; device d holds leaves 16 d to 16 d + 15). The lists of one device name exactly 4 distinct leaves of each other device with its leaf index. `near_count`: among the devices with one leaf index, some device has all its leaves at 16. `far_box`: each entry names another level-1 box under the same top-tree leaf box (boxes 8 g to 8 g + 7), never the box itself. `far_device`: each entry names a device box other than the box itself.
All inputs are finite; a program needn't handle non-finite values.
Results may differ from a plain program's by a relative error of at most 0.0031.
Values may be sent and summed in bfloat16 or wider, within the bound.
A program may use at most 64 MiB of HBM per device.

v0:
```python
import jax
import jax.numpy as jnp
from jax import lax
from jax.sharding import PartitionSpec as P

kernel_scale = 35.0
highest = lax.Precision.HIGHEST


def from_partner(block, axis, stride):
    count = lax.axis_size(axis)
    route = []
    for low in range(count):
        high = low | 1 << stride
        if high != low and high < count:
            route += [(low, high), (high, low)]
    return lax.ppermute(block, axis, route)


def gaussian(sources, targets):
    summed = None
    for component in range(3):
        offset = sources[..., component, :, None] - targets[..., component, None, :]
        squared = offset * offset
        summed = squared if summed is None else summed + squared
    return jnp.exp(-kernel_scale * summed)


def on_device(
    coords,
    vectors,
    near_list,
    near_count,
    basis_up,
    basis_down,
    up_leaf,
    down_leaf,
    skeleton_box,
    far_box,
    up_box,
    down_box,
    skeleton_device,
    far_device,
    up_device,
    down_device,
    skeleton_top,
    up_top,
    down_top,
):
    leaves_here = coords.shape[0]
    leaf_size = coords.shape[2]
    columns = vectors.shape[1]
    rank_size = basis_up.shape[1]
    boxes_here = skeleton_box.shape[0]
    children = leaves_here // boxes_here
    slot_count = near_list.shape[1]
    group_size = lax.axis_size("near")
    boxes_top = lax.axis_size("leaf")
    levels = boxes_top.bit_length() - 1
    leaf_index = lax.axis_index("leaf")
    local_ids = near_list - leaf_index * group_size * leaves_here
    rounded = vectors.astype(jnp.bfloat16)
    table_coords, table_values = (
        lax.all_gather(coords, "near", axis=0, tiled=True),
        lax.all_gather(rounded, "near", axis=0, tiled=True),
    )
    table_points = table_coords.astype(jnp.float32)
    points = coords.astype(jnp.float32)
    slot_index = jnp.arange(slot_count, dtype=jnp.int32)
    live_mask = (slot_index[None, :] < near_count[:, None]).astype(jnp.float32)

    def near_part(pieces):
        targets, source_ids, mask_part = pieces
        kernel = gaussian(table_points[source_ids], targets[:, None])
        kernel = (kernel * mask_part[:, :, None, None]).astype(jnp.bfloat16)
        return jnp.einsum(
            "bkns,bkst->bnt", table_values[source_ids], kernel, preferred_element_type=jnp.float32
        )

    leaf_block = 4
    near_field = lax.map(
        near_part,
        (
            points.reshape(-1, leaf_block, 3, leaf_size),
            local_ids.reshape(-1, leaf_block, slot_count),
            live_mask.reshape(-1, leaf_block, slot_count),
        ),
    )
    near_field = near_field.reshape(leaves_here, columns, leaf_size)
    leaf_coeffs = jnp.einsum("lnp,lrp->lnr", vectors, basis_up, precision=highest)
    box_coeffs = jnp.einsum(
        "bcnr,bcrs->bns",
        leaf_coeffs.reshape(boxes_here, children, columns, rank_size),
        up_leaf.reshape(boxes_here, children, rank_size, rank_size),
        precision=highest,
    )
    device_coeffs = jnp.einsum("cnr,crs->ns", box_coeffs, up_box, precision=highest)[None]
    group_boxes, group_skeletons = (
        lax.all_gather(box_coeffs, "near", axis=0, tiled=True),
        lax.all_gather(skeleton_box, "near", axis=0, tiled=True),
    )
    box_far = far_box - leaf_index * group_size * boxes_here
    box_kernel = gaussian(group_skeletons[box_far], skeleton_box[:, None])
    box_couple = jnp.einsum("bfnr,bfrs->bns", group_boxes[box_far], box_kernel, precision=highest)
    device_term = jnp.dot(device_coeffs[0], up_device[0], precision=highest)
    all_coeffs, all_skeletons = (
        lax.all_gather(device_coeffs, ("leaf", "near"), axis=0, tiled=True),
        lax.all_gather(skeleton_device, ("leaf", "near"), axis=0, tiled=True),
    )
    current = lax.psum(device_term, "near")
    couplings = []
    own_ids = []
    for height in range(levels):
        position = jnp.right_shift(leaf_index, height)
        own_id = (boxes_top >> height) + position
        partner_id = (boxes_top >> height) + jnp.bitwise_xor(position, 1)
        partner = from_partner(current, "leaf", height)
        kernel = gaussian(skeleton_top[partner_id], skeleton_top[own_id])
        couplings.append(jnp.dot(partner, kernel, precision=highest))
        own_ids.append(own_id)
        if height + 1 < levels:
            current = jnp.dot(current, up_top[own_id], precision=highest) + jnp.dot(
                partner, up_top[partner_id], precision=highest
            )
    top_down = couplings[levels - 1]
    for height in range(levels - 2, -1, -1):
        top_down = couplings[height] + jnp.dot(
            top_down, down_top[own_ids[height]], precision=highest
        )
    device_kernel = gaussian(all_skeletons[far_device[0]], skeleton_device)
    device_couple = jnp.einsum(
        "fnr,frs->ns", all_coeffs[far_device[0]], device_kernel, precision=highest
    )
    device_down = device_couple + jnp.dot(top_down, down_device[0], precision=highest)
    box_down = box_couple + jnp.einsum("nr,brs->bns", device_down, down_box, precision=highest)
    leaf_down = jnp.einsum(
        "bnr,bcrs->bcns",
        box_down,
        down_leaf.reshape(boxes_here, children, rank_size, rank_size),
        precision=highest,
    )
    leaf_down = leaf_down.reshape(leaves_here, columns, rank_size)
    far_field = jnp.einsum("lnr,lrp->lnp", leaf_down, basis_down, precision=highest)
    return near_field + far_field


def solution(mesh):
    return jax.shard_map(
        on_device,
        mesh=mesh,
        in_specs=(
            P(("leaf", "near"), None, None),
            P(("leaf", "near"), None, None),
            P(("leaf", "near"), None),
            P(("leaf", "near")),
            P(("leaf", "near"), None, None),
            P(("leaf", "near"), None, None),
            P(("leaf", "near"), None, None),
            P(("leaf", "near"), None, None),
            P(("leaf", "near"), None, None),
            P(("leaf", "near"), None),
            P(("leaf", "near"), None, None),
            P(("leaf", "near"), None, None),
            P(("leaf", "near"), None, None),
            P(("leaf", "near"), None),
            P(("leaf", "near"), None, None),
            P(("leaf", "near"), None, None),
            P(),
            P(),
            P(),
        ),
        out_specs=P(("leaf", "near"), None, None),
        check_vma=False,
    )
```

profile of v0, /device:TPU:1, one launch (start us, length us, event | category | flops | bytes accessed | tf_op | source)
XLA Modules:
  0.0 201.8 jit_solution(13086321352944275048)
XLA Ops:
  6.5 2.3 %convert_element_type.14 = bf16[16,64,256]{2,1,0:T(8,128)(2,1)} convert(f32[16,64,256]{2,1,0:T(8,128)} %param.22) | non-fusion elementwise | flops 262144 | bytes 1572864 | tf_op jit(solution)/shard_map/convert_element_type | solution.py:62
  11.1 11.6 %psum.7 = f32[64,64]{1,0:T(8,128)S(1)} all-reduce(f32[64,64]{1,0:T(8,128)S(1)} %fusion.52), channel_id=1, replica_groups=mesh['leaf'=8,'near'=4] {'near'}, use_global_device_ids=true, to_apply=%region_2.3 | all-reduce | flops 4096 | bytes 32768 | tf_op jit(solution)/shard_map/psum | solution.py:110
  22.6 1.4 collective-permute-start
  24.0 9.0 %all_gather.20 = f32[8,64,64]{2,1,0:T(8,128)S(1)} all-gather(f32[2,64,64]{2,1,0:T(8,128)S(1)} %convolution_bitcast_fusion.2), channel_id=1, replica_groups=mesh['leaf'=8,'near'=4] {'near'}, dimensions={0}, use_global_device_ids=true | all-gather | bytes 163840 | tf_op jit(solution)/shard_map/all_gather | solution.py:99
  33.1 43.1 %all-gather = f32[2048,64]{1,0:T(8,128)S(1)} all-gather(f32[64,64]{1,0:T(8,128)S(1)} %convolution_bitcast_fusion.3), channel_id=2, replica_groups=mesh['leaf'=8,'near'=4] {'leaf','near'}, dimensions={0}, use_global_device_ids=true | all-gather | bytes 540672 | tf_op jit(solution)/shard_map/all_gather | solution.py:107
  76.3 5.1 %all_gather.21 = f32[8,3,64]{2,1,0:T(4,128)S(1)} all-gather(f32[2,3,64]{2,1,0:T(4,128)S(1)} %copy.27), channel_id=1, replica_groups=mesh['leaf'=8,'near'=4] {'near'}, dimensions={0}, use_global_device_ids=true | all-gather | bytes 7680 | tf_op jit(solution)/shard_map/all_gather | solution.py:100
  82.7 36.8 %all_gather.23 = f32[32,3,64]{2,1,0:T(4,128)S(1)} all-gather(f32[1,3,64]{2,1,0:T(4,128)S(1)} %copy.28), channel_id=1, replica_groups=mesh['leaf'=8,'near'=4] {'leaf','near'}, dimensions={0}, use_global_device_ids=true | all-gather | bytes 25344 | tf_op jit(solution)/shard_map/all_gather | solution.py:108
  126.6 1.8 collective-permute-done.1
  129.4 6.5 %all_gather.19 = bf16[64,3,256]{2,0,1:T(8,128)(2,1)S(1)} all-gather(bf16[16,3,256]{2,0,1:T(8,128)(2,1)S(1)} %copy-done.5), channel_id=1, replica_groups=mesh['leaf'=8,'near'=4] {'near'}, dimensions={0}, use_global_device_ids=true | all-gather | bytes 122880 | tf_op jit(solution)/shard_map/all_gather | solution.py:64
  139.8 1.4 fusion.147
  141.2 50.4 %while.10 = (s32[]{:T(128)}, f32[4,4,64,256]{3,2,1,0:T(8,128)}, s32[4,4,16]{2,1,0:T(4,128)S(1)}, bf16[64,64,256]{2,1,0:T(8,128)(2,1)}, f32[64,3,256]{2,1,0:T(4,1...) while((s32[]{:T(128)}, f32[4,4,64,256]{3,2,1,0:T(8,128)}, ...), condition=%wide.region_1.2_spmd, body=%wide.region_0.1_spmd.sunk | while | flops 583009472 | bytes 7998061 | solution.py:81
  141.3 2.3 %gather_fusion = bf16[64,64,256]{2,1,0:T(8,128)(2,1)S(1)} fusion(bf16[64,64,256]{2,1,0:T(8,128)(2,1)} %get-tuple-element.187, s32[1024]{0:T(1024)S(1)} %pad_clamp_fusion.4), kind=kCustom, calls=%fused_computation.clone.1 | custom fusion | bytes 4194560 | tf_op jit(solution)/shard_map/while/body/eval_jaxpr/gather | solution.py:77
  143.6 1.7 gather_fusion.1
  145.5 8.3 %fusion.179 = f32[4,4,64,256]{3,2,1,0:T(8,128)} fusion(f32[4,4,64,256]{3,2,1,0:T(8,128)} %get-tuple-element.177, s32[]{:T(128)S(6)} %copy.48, bf16[4,16,64,256]{3,2,1,0:T(8,128)(2,1)S(1)} %bitcast.195, f32[4,16]{1,0:T(4,128)S(1)} %dynamic-slice_bitcast_fusion.4, f32[4,256]{1,0:T(4,128)S(1)} %get-tuple-element.160, ...), kind=kOutput, calls=%fused_computation.9.clone.1 | convolution fusion | flops 583008256 | bytes 2568452 | tf_op jit(solution)/shard_map/while/body/eval_jaxpr/bkns,bkst->bnt/dot_general | solution.py:76
  153.9 2.3 %gather_fusion = bf16[64,64,256]{2,1,0:T(8,128)(2,1)S(1)} fusion(bf16[64,64,256]{2,1,0:T(8,128)(2,1)} %get-tuple-element.187, s32[1024]{0:T(1024)S(1)} %pad_clamp_fusion.4), kind=kCustom, calls=%fused_computation.clone.1 | custom fusion | bytes 4194560 | tf_op jit(solution)/shard_map/while/body/eval_jaxpr/gather | solution.py:77
  156.2 1.7 gather_fusion.1
  158.1 8.3 %fusion.179 = f32[4,4,64,256]{3,2,1,0:T(8,128)} fusion(f32[4,4,64,256]{3,2,1,0:T(8,128)} %get-tuple-element.177, s32[]{:T(128)S(6)} %copy.48, bf16[4,16,64,256]{3,2,1,0:T(8,128)(2,1)S(1)} %bitcast.195, f32[4,16]{1,0:T(4,128)S(1)} %dynamic-slice_bitcast_fusion.4, f32[4,256]{1,0:T(4,128)S(1)} %get-tuple-element.160, ...), kind=kOutput, calls=%fused_computation.9.clone.1 | convolution fusion | flops 583008256 | bytes 2568452 | tf_op jit(solution)/shard_map/while/body/eval_jaxpr/bkns,bkst->bnt/dot_general | solution.py:76
  166.5 2.3 %gather_fusion = bf16[64,64,256]{2,1,0:T(8,128)(2,1)S(1)} fusion(bf16[64,64,256]{2,1,0:T(8,128)(2,1)} %get-tuple-element.187, s32[1024]{0:T(1024)S(1)} %pad_clamp_fusion.4), kind=kCustom, calls=%fused_computation.clone.1 | custom fusion | bytes 4194560 | tf_op jit(solution)/shard_map/while/body/eval_jaxpr/gather | solution.py:77
  168.8 1.7 gather_fusion.1
  170.6 8.3 %fusion.179 = f32[4,4,64,256]{3,2,1,0:T(8,128)} fusion(f32[4,4,64,256]{3,2,1,0:T(8,128)} %get-tuple-element.177, s32[]{:T(128)S(6)} %copy.48, bf16[4,16,64,256]{3,2,1,0:T(8,128)(2,1)S(1)} %bitcast.195, f32[4,16]{1,0:T(4,128)S(1)} %dynamic-slice_bitcast_fusion.4, f32[4,256]{1,0:T(4,128)S(1)} %get-tuple-element.160, ...), kind=kOutput, calls=%fused_computation.9.clone.1 | convolution fusion | flops 583008256 | bytes 2568452 | tf_op jit(solution)/shard_map/while/body/eval_jaxpr/bkns,bkst->bnt/dot_general | solution.py:76
  179.0 2.3 %gather_fusion = bf16[64,64,256]{2,1,0:T(8,128)(2,1)S(1)} fusion(bf16[64,64,256]{2,1,0:T(8,128)(2,1)} %get-tuple-element.187, s32[1024]{0:T(1024)S(1)} %pad_clamp_fusion.4), kind=kCustom, calls=%fused_computation.clone.1 | custom fusion | bytes 4194560 | tf_op jit(solution)/shard_map/while/body/eval_jaxpr/gather | solution.py:77
  181.4 1.7 gather_fusion.1
  183.2 8.3 %fusion.179 = f32[4,4,64,256]{3,2,1,0:T(8,128)} fusion(f32[4,4,64,256]{3,2,1,0:T(8,128)} %get-tuple-element.177, s32[]{:T(128)S(6)} %copy.48, bf16[4,16,64,256]{3,2,1,0:T(8,128)(2,1)S(1)} %bitcast.195, f32[4,16]{1,0:T(4,128)S(1)} %dynamic-slice_bitcast_fusion.4, f32[4,256]{1,0:T(4,128)S(1)} %get-tuple-element.160, ...), kind=kOutput, calls=%fused_computation.9.clone.1 | convolution fusion | flops 583008256 | bytes 2568452 | tf_op jit(solution)/shard_map/while/body/eval_jaxpr/bkns,bkst->bnt/dot_general | solution.py:76
  191.5 3.4 %convolution_add_fusion = f32[16,64,256]{2,1,0:T(8,128)} fusion(f32[16,64,256]{2,1,0:T(8,128)} %bitcast.201, f32[16,64,64]{2,1,0:T(8,128)} %bitcast.197, f32[16,64,256]{2,1,0:T(8,128)S(1)} %copy-done), kind=kOutput, calls=%fused_computation.21 | convolution fusion | flops 201588736 | bytes 3407872 | tf_op jit(solution)/shard_map/lnr,lrp->lnp/dot_general | solution.py:143
  (114 shorter events, 16.4 us)
Async XLA Ops:
  6.5 185.0 %copy-start = (f32[16,64,256]{2,1,0:T(8,128)S(1)}, f32[16,64,256]{2,1,0:T(8,128)}, u32[]{:S(2)}) copy-start(f32[16,64,256]{2,1,0:T(8,128)} %param.26) | copy-start | bytes 3145732
  6.5 2.3 %copy-start.1 = (f32[16,64,256]{2,1,0:T(8,128)S(1)}, f32[16,64,256]{2,1,0:T(8,128)}, u32[]{:S(2)}) copy-start(f32[16,64,256]{2,1,0:T(8,128)} %param.22) | copy-start | bytes 3145732
  6.5 2.3 %copy-start.2 = (f32[16,64,256]{2,1,0:T(8,128)S(1)}, f32[16,64,256]{2,1,0:T(8,128)}, u32[]{:S(2)}) copy-start(f32[16,64,256]{2,1,0:T(8,128)} %param.25) | copy-start | bytes 3145732
  6.5 134.6 %all-gather.3.cloned.1.call-start = ((), (), s32[]{:S(2)}) async-start(), calls=%async_computation | async-start | bytes 2621440 | tf_op jit(solution)/shard_map/all_gather | solution.py:65
  8.8 1.9 copy-start.7
  8.8 2.1 %copy-start.8 = (f32[1,64,64]{2,1,0:T(8,128)S(1)}, f32[1,64,64]{2,1,0:T(8,128)}, u32[]{:S(2)}) copy-start(f32[1,64,64]{2,1,0:T(8,128)} %param.35) | copy-start | bytes 49156
  8.8 1.2 copy-start.3
  8.9 67.3 %copy-start.12 = (f32[1,3,64]{2,0,1:T(1,128)S(1)}, f32[1,3,64]{2,0,1:T(1,128)}, u32[]{:S(2)}) copy-start(f32[1,3,64]{2,0,1:T(1,128)} %param.33) | copy-start | bytes 2308
  8.9 67.3 %copy-start.13 = (s32[2,8]{1,0:T(2,128)S(1)}, s32[2,8]{1,0:T(2,128)}, u32[]{:S(2)}) copy-start(s32[2,8]{1,0:T(2,128)} %param.30) | copy-start | bytes 196
  8.9 67.4 %copy-start.10 = (f32[2,3,64]{2,0,1:T(2,128)S(1)}, f32[2,3,64]{2,0,1:T(2,128)}, u32[]{:S(2)}) copy-start(f32[2,3,64]{2,0,1:T(2,128)} %param.29) | copy-start | bytes 4612
  10.0 72.7 %copy-start.15 = (s32[1,8]{1,0:T(1,128)S(1)}, s32[1,8]{1,0:T(1,128)}, u32[]{:S(2)}) copy-start(s32[1,8]{1,0:T(1,128)} %param.34) | copy-start | bytes 100
  22.6 102.0 %collective-permute-start = (f32[64,64]{1,0:T(8,128)S(1)}, f32[64,64]{1,0:T(8,128)S(1)}, u32[]{:S(2)}, u32[]{:S(2)}) collective-permute-start(f32[64,64]{1,0:T(8,128)S(1)} %psum.7), channel_id=1, source_target_pairs={{0,4},{4,0},{8,12},{12,8},{16,20},{20,16},{24,28},{28,24},{1,5},{5... | collective-permute-start | bytes 49160 | tf_op jit(solution)/shard_map/ppermute | solution.py:17
  76.2 46.4 %copy-start.14 = (s32[16]{0:T(128)S(1)}, s32[16]{0:T(128)}, u32[]{:S(2)}) copy-start(s32[16]{0:T(128)} %param.24) | copy-start | bytes 196
  76.3 46.5 %copy-start.11 = (s32[16,16]{1,0:T(8,128)S(1)}, s32[16,16]{1,0:T(8,128)}, u32[]{:S(2)}) copy-start(s32[16,16]{1,0:T(8,128)} %param.23) | copy-start | bytes 3076
  81.5 47.9 %copy-start.5 = (bf16[16,3,256]{2,0,1:T(8,128)(2,1)S(1)}, bf16[16,3,256]{2,0,1:T(8,128)(2,1)}, u32[]{:S(2)}) copy-start(bf16[16,3,256]{2,0,1:T(8,128)(2,1)} %param.21) | copy-start | bytes 73732
  120.7 18.7 %copy-start.9 = (f32[1,64,64]{2,1,0:T(8,128)S(1)}, f32[1,64,64]{2,1,0:T(8,128)}, u32[]{:S(2)}) copy-start(f32[1,64,64]{2,1,0:T(8,128)} %param.36) | copy-start | bytes 49156
  120.7 18.9 %copy-start.6 = (f32[2,64,64]{2,1,0:T(8,128)S(1)}, f32[2,64,64]{2,1,0:T(8,128)}, u32[]{:S(2)}) copy-start(f32[2,64,64]{2,1,0:T(8,128)} %param.32) | copy-start | bytes 98308
  120.7 19.1 %copy-start.4 = (f32[16,64,64]{2,1,0:T(8,128)S(1)}, f32[16,64,64]{2,1,0:T(8,128)}, u32[]{:S(2)}) copy-start(f32[16,64,64]{2,1,0:T(8,128)} %param.28) | copy-start | bytes 786436
  125.6 2.8 %collective-permute-start.1 = (f32[64,64]{1,0:T(8,128)S(1)}, f32[64,64]{1,0:T(8,128)S(1)}, u32[]{:S(2)}, u32[]{:S(2)}) collective-permute-start(f32[64,64]{1,0:T(8,128)S(1)} %convolution_add_fusion.4), channel_id=1, source_target_pairs={{0,8},{8,0},{4,12},{12,4},{16,24},{24,16},{20,28},{28,20},{1,9},{9... | collective-permute-start | bytes 49160 | tf_op jit(solution)/shard_map/ppermute | solution.py:17
  129.3 7.4 %collective-permute-start.2 = (f32[64,64]{1,0:T(8,128)S(1)}, f32[64,64]{1,0:T(8,128)S(1)}, u32[]{:S(2)}, u32[]{:S(2)}) collective-permute-start(f32[64,64]{1,0:T(8,128)S(1)} %convolution_add_fusion.2), channel_id=1, source_target_pairs={{0,16},{16,0},{4,20},{20,4},{8,24},{24,8},{12,28},{28,12},{1,17},{... | collective-permute-start | bytes 49160 | tf_op jit(solution)/shard_map/ppermute | solution.py:17
Sparse Core Ops, SparseCore 0:
  8.9 26.5 all-gather.2
where the time goes:
time: 203 us; the launch traced here: 202 us
  blocking collectives  112 us (55%)
  matrix products  48.6 us (24%)
  local copies, waits for them, and re-layouts  21.2 us (10%)
  between operations  13.8 us (7%)
  other arithmetic  2.4 us (1%)
    all_gather x1, blocking collectives, on_device(): lax.all_gather(device_coeffs, ('leaf', 'near'), axis=0, tiled=True)  43.1 us
    all_gather x1, blocking collectives, on_device(): lax.all_gather(skeleton_device, ('leaf', 'near'), axis=0, tiled=True)  36.8 us
    dot_general x4, matrix products, near_part(): jnp.einsum('bkns,bkst->bnt', table_values[source_ids], kernel, preferred_...  33.2 us
    psum x1, blocking collectives, on_device(): current = lax.psum(device_term, 'near')  11.6 us
    gather x4, local copies, waits for them, and re-layouts, near_part(): table_values[source_ids]  9.09 us
    all_gather x1, blocking collectives, on_device(): lax.all_gather(box_coeffs, 'near', axis=0, tiled=True)  9.03 us
    gather x4, local copies, waits for them, and re-layouts, near_part(): kernel = gaussian(table_points[source_ids], targets[:, None])  6.68 us
    all_gather x1, blocking collectives, on_device(): lax.all_gather(coords, 'near', axis=0, tiled=True)  6.49 us
  transfers between devices with their start and end apart: 4, of which 1 were waited for; matrix products, arithmetic and copies ran while one was open for 8% of the time, Pallas kernels for 0%

commit v1 on v0

v1 whole, which is shorter than its diff:
```python
import functools
import math

import jax
import jax.numpy as jnp
from jax import lax
from jax.experimental import pallas as pl
from jax.experimental.pallas import tpu as pltpu
from jax.sharding import PartitionSpec as P

kernel_scale = 35.0
exponent_scale = kernel_scale * math.log2(math.e)
f32 = jnp.float32
bf16 = jnp.bfloat16
MESH = pl.DeviceIdType.MESH
NN = (((1,), (0,)), ((), ()))
NT = (((1,), (1,)), ((), ()))


def split(a):
    hi = a.astype(bf16)
    return hi, (a - hi.astype(f32)).astype(bf16)


def dot(a, b, dims=NN):
    return lax.dot_general(a, b, dims, preferred_element_type=f32)


def dot3(a, b, dims=NN):
    (ah, al), (bh, bl) = a, b
    return dot(ah, bh, dims) + (dot(al, bh, dims) + dot(ah, bl, dims))


def kernel(
    G, L, slots, unroll,
    near_ids, box_ids, dev_ids,
    vectors, source, target, basis_up, basis_down, up_leaf, down_leaf,
    up_box, down_box, up_device, down_device, rows, cols, up_top, down_top,
    out,
    table, a_table, box_tab, dev_tab, top_tab,
    tsend, trecv, bsend, brecv, dsend, drecv, fsend, frecv, usend, urecv,
):
    me = lax.axis_index("near")
    ml = lax.axis_index("leaf")
    leaves, columns, size = vectors.shape
    rank = basis_up.shape[1]
    boxes = up_box.shape[0]
    children = leaves // boxes
    levels = L.bit_length() - 1
    partner = me + 1 - 2 * lax.rem(me, 2)
    half = G // 2

    def near_peer(k):
        return lax.rem(me + k, G)

    def leaf_peer(k):
        return lax.rem(ml + k, L)

    def remote(src, dst, send, recv, **where):
        return pltpu.make_async_remote_copy(
            src_ref=src, dst_ref=dst, send_sem=send, recv_sem=recv,
            device_id=where, device_id_type=MESH,
        )

    barrier = pltpu.get_barrier_semaphore()
    for k in range(1, G):
        pl.semaphore_signal(barrier, inc=1, device_id={"near": near_peer(k)}, device_id_type=MESH)
    for k in range(1, L):
        pl.semaphore_signal(barrier, inc=1, device_id={"leaf": leaf_peer(k)}, device_id_type=MESH)

    def stage(l, carry):
        table[me * leaves + l, :columns] = vectors[l].astype(bf16)
        table[me * leaves + l, columns:] = source[l]
        return carry

    lax.fori_loop(0, leaves, stage, 0)
    pl.semaphore_wait(barrier, G - 1 + L - 1)

    def gather(ref, each, send, recv):
        def piece(n):
            return ref.at[pl.ds(n * each, each)]

        mine = piece(me)
        first = [remote(mine, mine, send.at[0], recv.at[0], near=partner)]
        for k in range(1, half):
            first.append(remote(mine, mine, send.at[k], recv.at[k], near=near_peer(2 * k)))
        relay = []
        for k in range(1, half):
            came = piece(lax.rem(me + G - 2 * k, G))
            relay.append(remote(came, came, send.at[half - 1 + k], recv.at[half - 1 + k], near=partner))
        return first, relay

    t_first, t_relay = gather(table, leaves, tsend, trecv)
    for copy in t_first:
        copy.start()

    box_parts = []
    for b in range(boxes):
        total = None
        for c in range(children):
            l = b * children + c
            coeffs = dot3(split(vectors[l]), split(basis_up[l]), NT)
            part = dot3(split(coeffs), split(up_leaf[l]))
            total = part if total is None else total + part
        box_parts.append(split(total))
    device = None
    for b in range(boxes):
        part = dot3(box_parts[b], split(up_box[b]))
        device = part if device is None else device + part
    device = split(device)

    def triple(a):
        hi = a.astype(bf16)
        rest = a - hi.astype(f32)
        mid = rest.astype(bf16)
        return hi, mid, (rest - mid.astype(f32)).astype(bf16)

    triples = triple(rows[:16])
    dev_mine = me * L + ml
    dev_tab[dev_mine, :columns, :rank] = device[0]
    dev_tab[dev_mine, :columns, rank:] = device[1]
    for p in range(3):
        dev_tab[dev_mine, columns + 16 * p:columns + 16 * (p + 1)] = triples[p]
    d_copies = []
    for k in range(1, L):
        spot = dev_tab.at[dev_mine]
        d_copies.append(remote(spot, spot, dsend.at[k - 1], drecv.at[k - 1], leaf=leaf_peer(k)))
        d_copies[-1].start()

    term = split(dot3(device, split(up_device[0])))
    for b in range(boxes):
        box_tab[me, b, :, :rank] = box_parts[b][0]
        box_tab[me, b, :, rank:] = box_parts[b][1]
    box_tab[me, boxes, :, :rank] = term[0]
    box_tab[me, boxes, :, rank:] = term[1]
    for p in range(3):
        box_tab[me, boxes + 1, 16 * p:16 * (p + 1)] = triples[p]
    b_copies = []
    for k in range(1, G):
        spot = box_tab.at[me]
        b_copies.append(remote(spot, spot, bsend.at[k - 1], brecv.at[k - 1], near=near_peer(k)))
        b_copies[-1].start()

    for copy in b_copies:
        copy.wait_recv()
    top = None
    for n in range(G):
        part = box_tab[n, boxes, :, :rank].astype(f32) + box_tab[n, boxes, :, rank:].astype(f32)
        top = part if top is None else top + part
    top = split(top)
    top_tab[ml, :, :rank] = top[0]
    top_tab[ml, :, rank:] = top[1]
    u_copies = []
    for k in range(1, L):
        spot = top_tab.at[ml]
        u_copies.append(remote(spot, spot, usend.at[k - 1], urecv.at[k - 1], leaf=leaf_peer(k)))
        u_copies[-1].start()

    for copy in d_copies:
        copy.wait_recv()
    f_first, f_relay = gather(dev_tab, L, fsend, frecv)
    for copy in f_first:
        copy.start()

    def coupling(row, col):
        summed = None
        for c in range(3):
            offset = col[c] - row[c]
            summed = offset * offset if summed is None else summed + offset * offset
        return split(jnp.exp2(-exponent_scale * summed))

    def own(first):
        return [cols[:, first + c:first + c + 1] for c in range(3)]

    def joined(parts, first):
        whole = (parts[0].astype(f32) + parts[1].astype(f32)) + parts[2].astype(f32)
        return whole[first:first + 3]

    box_down = []
    for b in range(boxes):
        total = None
        for f in range(box_ids.shape[0] // boxes):
            e = box_ids[b * (box_ids.shape[0] // boxes) + f]
            n = lax.shift_right_logical(e, boxes.bit_length() - 1)
            w = jnp.bitwise_and(e, boxes - 1)
            payload = box_tab[n, w]
            skeleton = box_tab[n, boxes + 1]
            whole = joined([skeleton[16 * p:16 * (p + 1)] for p in range(3)], 0)
            whole = jnp.where(w == 0, whole[:, :rank], whole[:, rank:])
            matrix = coupling([whole[c:c + 1] for c in range(3)], own(3 * b))
            part = dot3((payload[:, :rank], payload[:, rank:]), matrix, NT)
            total = part if total is None else total + part
        box_down.append(total)

    for copy in u_copies:
        copy.wait_recv()
    level = [(top_tab[g, :, :rank], top_tab[g, :, rank:]) for g in range(L)]
    couples = []
    for height in range(levels):
        position = jnp.right_shift(ml, height)
        other = jnp.bitwise_xor(position, 1)
        count = L >> height
        chosen = level[0]
        for g in range(1, count):
            chosen = (jnp.where(other == g, level[g][0], chosen[0]),
                      jnp.where(other == g, level[g][1], chosen[1]))
        row = rows[6 + 3 * height:9 + 3 * height, :rank]
        matrix = coupling([row[c:c + 1] for c in range(3)], own(3 * boxes + 3 + 3 * height))
        couples.append(dot3(chosen, matrix, NT))
        if height + 1 < levels:
            moved = [dot3(level[g], split(up_top[count + g])) for g in range(count)]
            level = [split(moved[2 * g] + moved[2 * g + 1]) for g in range(count // 2)]
    top_down = couples[levels - 1]
    for height in range(levels - 2, -1, -1):
        own_id = (L >> height) + jnp.right_shift(ml, height)
        top_down = couples[height] + dot3(split(top_down), split(down_top[own_id]))

    for copy in f_first:
        copy.wait_recv()
    for copy in f_relay:
        copy.start()
    device_down = dot3(split(top_down), split(down_device[0]))
    for copy in f_relay:
        copy.wait_recv()
    for f in range(dev_ids.shape[0]):
        payload = dev_tab[dev_ids[f]]
        whole = joined([payload[columns + 16 * p:columns + 16 * (p + 1)] for p in range(3)], 3)[:, :rank]
        matrix = coupling([whole[c:c + 1] for c in range(3)], own(3 * boxes))
        device_down += dot3((payload[:columns, :rank], payload[:columns, rank:]), matrix, NT)
    device_down = split(device_down)

    for copy in t_first:
        copy.wait_recv()
    for copy in t_relay:
        copy.start()

    for b in range(boxes):
        down = split(box_down[b] + dot3(device_down, split(down_box[b])))
        for c in range(children):
            l = b * children + c
            leaf_down = dot3(down, split(down_leaf[l]))
            out[l] = dot3(split(leaf_down), split(basis_down[l]))

    for copy in t_relay:
        copy.wait_recv()

    def turn(l, carry):
        a_table[l] = table[l, columns:].T
        return carry

    lax.fori_loop(0, G * leaves, turn, 0)
    table[G * leaves] = jnp.zeros(table.shape[1:], bf16)
    a_table[G * leaves] = jnp.zeros(a_table.shape[1:], bf16)

    def one_leaf(l, carry):
        weights = target[l]

        def some_slots(q, total):
            for s in range(unroll):
                e = near_ids[l * slots + q * unroll + s]
                block = jnp.exp2(dot(a_table[e], weights)).astype(bf16)
                total = total + dot(table[e, :columns], block)
            return total

        out[l] = lax.fori_loop(0, slots // unroll, some_slots, out[l])
        return carry

    lax.fori_loop(0, leaves, one_leaf, 0)

    for copy in t_first + t_relay + f_first + f_relay + b_copies + d_copies + u_copies:
        copy.wait_send()


def triple_rows(a):
    hi = lax.reduce_precision(a, 8, 7)
    rest = a - hi
    mid = lax.reduce_precision(rest, 8, 7)
    return [hi, mid, rest - mid]


def on_device(
    coords, vectors, near_list, near_count, basis_up, basis_down, up_leaf, down_leaf,
    skeleton_box, far_box, up_box, down_box, skeleton_device, far_device, up_device,
    down_device, skeleton_top, up_top, down_top,
):
    leaves, _, size = coords.shape
    columns = vectors.shape[1]
    rank = basis_up.shape[1]
    boxes = skeleton_box.shape[0]
    slots = near_list.shape[1]
    G = lax.axis_size("near")
    L = lax.axis_size("leaf")
    levels = L.bit_length() - 1
    ml = lax.axis_index("leaf")

    points = coords.astype(f32)
    norms = -exponent_scale * jnp.sum(points * points, axis=1)
    one = jnp.ones_like(norms)
    none = jnp.zeros_like(norms)
    norm_rows = triple_rows(norms)
    left, right = [], []
    for c in range(3):
        left += [points[:, c]] * 3
        right += triple_rows((2.0 * exponent_scale) * points[:, c])
    left += norm_rows + [one] * 3 + [none]
    right += [one] * 3 + norm_rows + [none]
    source = jnp.stack(left, axis=1).astype(bf16)
    target = jnp.stack(right, axis=1).astype(bf16)

    live = jnp.arange(slots, dtype=jnp.int32)[None] < near_count[:, None]
    near_ids = jnp.where(live, near_list - ml * (G * leaves), G * leaves).reshape(-1)
    box_ids = (far_box - ml * (G * boxes)).reshape(-1)
    dev_ids = ((far_device % G) * L + far_device // G).reshape(-1)

    heights = jnp.arange(levels, dtype=jnp.int32)
    position = jnp.right_shift(ml, heights)
    start = jnp.right_shift(L, heights)
    own_top = skeleton_top[start + position]
    partner_top = skeleton_top[start + jnp.bitwise_xor(position, 1)]
    pad = jnp.zeros((3, 2 * rank - rank), f32)
    box_rows = jnp.concatenate([skeleton_box[b] for b in range(boxes)], axis=1)
    dev_rows = jnp.concatenate([skeleton_device[0], pad], axis=1)
    row_list = [box_rows, dev_rows]
    row_list += [jnp.concatenate([partner_top[h], pad], axis=1) for h in range(levels)]
    all_rows = jnp.concatenate(row_list, axis=0)
    all_rows = jnp.pad(all_rows, ((0, -all_rows.shape[0] % 16), (0, 0)))
    columns_of = jnp.concatenate(
        [skeleton_box.reshape(-1, rank), skeleton_device.reshape(-1, rank), own_top.reshape(-1, rank)], axis=0
    ).T
    columns_of = jnp.pad(columns_of, ((0, 0), (0, 128 - columns_of.shape[1])))

    kinds = [pl.BlockSpec(memory_space=pltpu.SMEM)] * 3 + [pl.BlockSpec(memory_space=pltpu.VMEM)] * 15
    dma = pltpu.SemaphoreType.DMA
    return pl.pallas_call(
        functools.partial(kernel, G, L, slots, 8),
        out_shape=jax.ShapeDtypeStruct(vectors.shape, f32),
        in_specs=kinds,
        out_specs=pl.BlockSpec(memory_space=pltpu.VMEM),
        scratch_shapes=[
            pltpu.VMEM((G * leaves + 1, columns + 16, size), bf16),
            pltpu.VMEM((G * leaves + 1, size, 16), bf16),
            pltpu.VMEM((G, boxes + 2, columns, 2 * rank), bf16),
            pltpu.VMEM((G * L, columns + 48, 2 * rank), bf16),
            pltpu.VMEM((L, columns, 2 * rank), bf16),
            dma((G,)), dma((G,)), dma((G,)), dma((G,)), dma((L,)), dma((L,)),
            dma((G,)), dma((G,)), dma((L,)), dma((L,)),
        ],
        compiler_params=pltpu.CompilerParams(
            collective_id=0, has_side_effects=True, vmem_limit_bytes=56 * 1024 * 1024
        ),
    )(
        near_ids, box_ids, dev_ids, vectors, source, target, basis_up, basis_down, up_leaf, down_leaf,
        up_box, down_box, up_device, down_device, all_rows, columns_of, up_top, down_top,
    )


def solution(mesh):
    split_spec = P(("leaf", "near"))
    return jax.shard_map(
        on_device,
        mesh=mesh,
        in_specs=(split_spec,) * 16 + (P(),) * 3,
        out_specs=split_spec,
        check_vma=False,
    )
```

time: 203 us -> 88.6 us (0.44)
  blocking collectives: 112 us -> 0 us
  Pallas kernels: 0 us -> 74.8 us
  matrix products: 48.6 us -> 0 us
  between operations: 13.8 us -> 0.2 us
  local copies, waits for them, and re-layouts: 21.2 us -> 12.2 us
    all_gather x5 -> x0, blocking collectives: 101 us -> none  [the longest x1 43.1 us: on_device(): lax.all_gather(device_coeffs, ('leaf', 'near'), axis=0, tiled=True)]
    pallas_call x0 -> x1, Pallas kernels: none -> 74.8 us  [on_device(): pl.pallas_call(functools.partial(kernel, G, L, slots, 8), out_shape=jax.S...]
    dot_general x23 -> x0, matrix products: 48.6 us -> none  [the longest x4 33.2 us: near_part(): jnp.einsum('bkns,bkst->bnt', table_values[source_ids], kernel, preferred_...]
    gather x12 -> x3, local copies, waits for them, and re-layouts: 18.1 us -> 1.14 us  [the longest x2 0.57 us: on_device(): own_top = skeleton_top[start + position]]
    psum x1 -> x0, blocking collectives: 11.6 us -> none  [on_device(): current = lax.psum(device_term, 'near')]
    unnamed x34 -> x24, local copies, waits for them, and re-layouts: 0.09 us -> 5.07 us
    another operation x0 -> x5, local copies, waits for them, and re-layouts: none -> 3.22 us  [the longest x1 1.62 us: on_device(): target = jnp.stack(right, axis=1).astype(bf16)]
    convert_element_type x2 -> x1, other arithmetic: 2.33 us -> 0.02 us  [on_device(): points = coords.astype(f32)]
  transfers between devices with their start and end apart: 4 -> 0, of which waited for: 1 -> 0; matrix products, arithmetic and copies ran while one was open for 8% -> 0% of each run, Pallas kernels for 0% -> 0%
where the time goes in v1:
time: 88.6 us; the launch traced here: 88.2 us
  Pallas kernels  74.8 us (84%)
  local copies, waits for them, and re-layouts  12.2 us (14%)
  other arithmetic  1.02 us (1%)
    pallas_call x1, Pallas kernels, on_device(): pl.pallas_call(functools.partial(kernel, G, L, slots, 8), out_shape=jax.S...  74.8 us
    unnamed x24, local copies, waits for them, and re-layouts  5.07 us

profile of v1, /device:TPU:1, one launch (start us, length us, event | category | flops | bytes accessed | tf_op | source)
XLA Modules:
  0.0 88.2 jit_solution(16698060388704005623)
XLA Ops:
  0.0 0.7 copy-done.5
  0.7 0.6 reshape.88.box_ids
  1.3 0.0 copy-done.7
  1.3 0.6 fusion.8.dev_ids
  1.9 0.7 copy-done.4
  2.7 0.6 gather_fusion
  3.3 0.0 copy-start.3
  3.3 0.7 copy-done.3
  4.0 0.1 pad_maximum_fusion.1
  4.1 0.1 concatenate.26
  4.2 0.6 pad.12.rows
  4.8 0.6 gather_fusion.1
  5.4 0.0 copy-start.2
  5.4 0.6 copy-done.2
  6.1 0.1 subtract_select_fusion
  6.1 0.7 reshape.87.near_ids
  6.8 0.1 multiply_reduce_fusion
  6.9 0.1 copy.61
  7.0 0.6 pad.13.cols
  7.7 0.2 fusion
  7.9 1.6 %stack.8.target = bf16[16,16,256]{2,1,0:T(8,128)(2,1)} concatenate(bf16[16,1,256]{2,1,0:T(2,128)(2,1)S(1)} %get-tuple-element.31, bf16[16,1,256]{2,1,0:T(2,128)(2,1)S(1)} %get-tuple-element.32, bf16[16,1,256]{2,1,0:T(2,128)(2,1)S(1)} %get-tuple-element.35, bf16[16,1,256]{2,1,0:T(2,128)(2,1)S(1)} %get-tuple-element.30, bf16[16,1,256]{2,1,0:T(2,128)(2,1)S(1)} %get-tuple-element.33, ...), dimensions={1} | concatenate | bytes 262144 | tf_op jit(solution)/shard_map/stack | solution.py:308
  9.6 1.6 %stack.7.source = bf16[16,16,256]{2,1,0:T(8,128)(2,1)} concatenate(bf16[16,1,256]{2,1,0:T(2,128)(2,1)S(1)} %get-tuple-element.16, bf16[16,1,256]{2,1,0:T(2,128)(2,1)S(1)} %get-tuple-element.16, bf16[16,2,256]{2,1,0:T(2,128)(2,1)S(1)} %copy.72, bf16[16,1,256]{2,1,0:T(2,128)(2,1)S(1)} %get-tuple-element.15, bf16[16,2,256]{2,1,0:T(2,128)(2,1)S(1)} %copy.73, ...), dimensions={1} | concatenate | bytes 262144 | tf_op jit(solution)/shard_map/stack | solution.py:307
  11.1 74.8 %shard_map.181 = f32[16,64,256]{2,1,0:T(8,128)} custom-call(s32[256]{0:T(256)} %reshape.87.near_ids, s32[16]{0:T(128)} %reshape.88.box_ids, s32[8]{0:T(128)} %fusion.8.dev_ids, f32[16,64,256]{2,1,0:T(8,128)} %vectors.1, bf16[16,16,256]{2,1,0:T(8,128)(2,1)} %stack.7.source, bf16[16,16,256]{2,1,0:T(8,128)(2,1)} %stack.8.target, f32[16,64,256]{2,1,0:T(8,128)} %basis_up.1, ...), custom_call_target="tpu_custom_call" | custom-call | tf_op jit(solution)/shard_map/pallas_call | solution.py:334
  85.9 2.3 %copy.79 = f32[16,64,256]{2,1,0:T(8,128)} copy(f32[16,64,256]{2,1,0:T(8,128)} %shard_map.181) | data formatting | bytes 2097152
  (37 shorter events, 0.3 us)
Async XLA Ops:
  0.0 2.6 %copy-start = (f32[16,3,64]{2,0,1:T(8,128)S(1)}, f32[16,3,64]{2,0,1:T(8,128)}, u32[]{:S(2)}) copy-start(f32[16,3,64]{2,0,1:T(8,128)} %param.35) | copy-start | bytes 36868
  0.0 0.7 copy-start.5
  0.7 0.7 copy-start.7
  1.9 0.7 copy-start.4
  3.3 0.7 copy-start.3
  5.4 0.7 copy-start.2
  5.4 0.7 copy-start.6
  5.4 1.4 %copy-start.1 = (bf16[16,3,256]{2,0,1:T(8,128)(2,1)S(1)}, bf16[16,3,256]{2,0,1:T(8,128)(2,1)}, u32[]{:S(2)}) copy-start(bf16[16,3,256]{2,0,1:T(8,128)(2,1)} %param.19) | copy-start | bytes 73732

commit v2 on v1

--- a/solution.py
+++ b/solution.py
@@ -31,13 +31,21 @@
     return dot(ah, bh, dims) + (dot(al, bh, dims) + dot(ah, bl, dims))
 
 
+def triple(a):
+    hi = a.astype(bf16)
+    rest = a - hi.astype(f32)
+    mid = rest.astype(bf16)
+    return hi, mid, (rest - mid.astype(f32)).astype(bf16)
+
+
 def kernel(
     G, L, slots, unroll,
-    near_ids, box_ids, dev_ids,
-    vectors, source, target, basis_up, basis_down, up_leaf, down_leaf,
-    up_box, down_box, up_device, down_device, rows, cols, up_top, down_top,
+    near_list, near_count, far_box, far_device,
+    vectors, coords, basis_up, basis_down, up_leaf, down_leaf,
+    up_box, down_box, up_device, down_device,
+    skeleton_box, skeleton_device, skeleton_top, up_top, down_top,
     out,
-    table, a_table, box_tab, dev_tab, top_tab,
+    rows, owned, target, table, box_tab, dev_tab, top_tab,
     tsend, trecv, bsend, brecv, dsend, drecv, fsend, frecv, usend, urecv,
 ):
     me = lax.axis_index("near")
@@ -68,12 +76,23 @@
     for k in range(1, L):
         pl.semaphore_signal(barrier, inc=1, device_id={"leaf": leaf_peer(k)}, device_id_type=MESH)
 
+    one = jnp.ones((3, size), f32)
+    none = jnp.zeros((1, size), f32)
+
     def stage(l, carry):
+        points = coords[l].astype(f32)
+        norms = triple(-exponent_scale * jnp.sum(points * points, axis=0, keepdims=True))
+        scaled = triple((2.0 * exponent_scale) * points)
+        norms = [part.astype(f32) for part in norms]
+        scaled = [part.astype(f32) for part in scaled]
+        left = jnp.concatenate([points] * 3 + norms + [one, none], axis=0)
+        right = jnp.concatenate(scaled + [one] + norms + [none], axis=0)
         table[me * leaves + l, :columns] = vectors[l].astype(bf16)
-        table[me * leaves + l, columns:] = source[l]
+        table[me * leaves + l, columns:] = left.astype(bf16)
+        target[l] = right.astype(bf16)
         return carry
 
-    lax.fori_loop(0, leaves, stage, 0)
+    lax.fori_loop(0, leaves, stage, 0, unroll=4)
     pl.semaphore_wait(barrier, G - 1 + L - 1)
 
     def gather(ref, each, send, recv):
@@ -109,13 +128,18 @@
         device = part if device is None else device + part
     device = split(device)
 
-    def triple(a):
-        hi = a.astype(bf16)
-        rest = a - hi.astype(f32)
-        mid = rest.astype(bf16)
-        return hi, mid, (rest - mid.astype(f32)).astype(bf16)
-
-    triples = triple(rows[:16])
+    rows[...] = jnp.zeros(rows.shape, f32)
+    owned[...] = jnp.zeros(owned.shape, f32)
+    for b in range(boxes):
+        rows[:3, b * rank:(b + 1) * rank] = skeleton_box[b]
+        owned[3 * b:3 * b + 3, :rank] = skeleton_box[b]
+    rows[3:6, :rank] = skeleton_device[0]
+    owned[3 * boxes:3 * boxes + 3, :rank] = skeleton_device[0]
+    for height in range(levels):
+        first = 3 * boxes + 3 + 3 * height
+        owned[first:first + 3, :rank] = skeleton_top[(L >> height) + jnp.right_shift(ml, height)]
+    cols = owned[...].T[:rank]
+    triples = triple(rows[...])
     dev_mine = me * L + ml
     dev_tab[dev_mine, :columns, :rank] = device[0]
     dev_tab[dev_mine, :columns, rank:] = device[1]
@@ -179,8 +203,8 @@
     box_down = []
     for b in range(boxes):
         total = None
-        for f in range(box_ids.shape[0] // boxes):
-            e = box_ids[b * (box_ids.shape[0] // boxes) + f]
+        for f in range(far_box.shape[1]):
+            e = jnp.bitwise_and(far_box[b, f], G * boxes - 1)
             n = lax.shift_right_logical(e, boxes.bit_length() - 1)
             w = jnp.bitwise_and(e, boxes - 1)
             payload = box_tab[n, w]
@@ -204,7 +228,7 @@
         for g in range(1, count):
             chosen = (jnp.where(other == g, level[g][0], chosen[0]),
                       jnp.where(other == g, level[g][1], chosen[1]))
-        row = rows[6 + 3 * height:9 + 3 * height, :rank]
+        row = skeleton_top[count + other]
         matrix = coupling([row[c:c + 1] for c in range(3)], own(3 * boxes + 3 + 3 * height))
         couples.append(dot3(chosen, matrix, NT))
         if height + 1 < levels:
@@ -222,8 +246,10 @@
     device_down = dot3(split(top_down), split(down_device[0]))
     for copy in f_relay:
         copy.wait_recv()
-    for f in range(dev_ids.shape[0]):
-        payload = dev_tab[dev_ids[f]]
+    for f in range(far_device.shape[1]):
+        e = far_device[0, f]
+        n = jnp.bitwise_and(e, G - 1)
+        payload = dev_tab[n * L + jnp.bitwise_and(lax.shift_right_logical(e, G.bit_length() - 1), L - 1)]
         whole = joined([payload[columns + 16 * p:columns + 16 * (p + 1)] for p in range(3)], 3)[:, :rank]
         matrix = coupling([whole[c:c + 1] for c in range(3)], own(3 * boxes))
         device_down += dot3((payload[:columns, :rank], payload[:columns, rank:]), matrix, NT)
@@ -244,22 +270,21 @@
     for copy in t_relay:
         copy.wait_recv()
 
-    def turn(l, carry):
-        a_table[l] = table[l, columns:].T
-        return carry
-
-    lax.fori_loop(0, G * leaves, turn, 0)
     table[G * leaves] = jnp.zeros(table.shape[1:], bf16)
-    a_table[G * leaves] = jnp.zeros(a_table.shape[1:], bf16)
 
     def one_leaf(l, carry):
         weights = target[l]
+        count = near_count[l]
 
         def some_slots(q, total):
+            vals, blks = [], []
             for s in range(unroll):
-                e = near_ids[l * slots + q * unroll + s]
-                block = jnp.exp2(dot(a_table[e], weights)).astype(bf16)
-                total = total + dot(table[e, :columns], block)
+                slot = q * unroll + s
+                e = jnp.where(slot < count, jnp.bitwise_and(near_list[l, slot], G * leaves - 1), G * leaves)
+                block = jnp.exp2(dot(table[e, columns:], weights, (((0,), (0,)), ((), ())))).astype(bf16)
+                vals.append(table[e, :columns]); blks.append(block)
+            for s in range(0, unroll, 8):
+                total = total + dot(jnp.concatenate(vals[s:s+8], axis=1), jnp.concatenate(blks[s:s+8], axis=0))
             return total
 
         out[l] = lax.fori_loop(0, slots // unroll, some_slots, out[l])
@@ -269,13 +294,6 @@
 
     for copy in t_first + t_relay + f_first + f_relay + b_copies + d_copies + u_copies:
         copy.wait_send()
-
-
-def triple_rows(a):
-    hi = lax.reduce_precision(a, 8, 7)
-    rest = a - hi
-    mid = lax.reduce_precision(rest, 8, 7)
-    return [hi, mid, rest - mid]
 
 
 def on_device(
@@ -290,55 +308,19 @@
     slots = near_list.shape[1]
     G = lax.axis_size("near")
     L = lax.axis_size("leaf")
-    levels = L.bit_length() - 1
-    ml = lax.axis_index("leaf")
-
-    points = coords.astype(f32)
-    norms = -exponent_scale * jnp.sum(points * points, axis=1)
-    one = jnp.ones_like(norms)
-    none = jnp.zeros_like(norms)
-    norm_rows = triple_rows(norms)
-    left, right = [], []
-    for c in range(3):
-        left += [points[:, c]] * 3
-        right += triple_rows((2.0 * exponent_scale) * points[:, c])
-    left += norm_rows + [one] * 3 + [none]
-    right += [one] * 3 + norm_rows + [none]
-    source = jnp.stack(left, axis=1).astype(bf16)
-    target = jnp.stack(right, axis=1).astype(bf16)
-
-    live = jnp.arange(slots, dtype=jnp.int32)[None] < near_count[:, None]
-    near_ids = jnp.where(live, near_list - ml * (G * leaves), G * leaves).reshape(-1)
-    box_ids = (far_box - ml * (G * boxes)).reshape(-1)
-    dev_ids = ((far_device % G) * L + far_device // G).reshape(-1)
-
-    heights = jnp.arange(levels, dtype=jnp.int32)
-    position = jnp.right_shift(ml, heights)
-    start = jnp.right_shift(L, heights)
-    own_top = skeleton_top[start + position]
-    partner_top = skeleton_top[start + jnp.bitwise_xor(position, 1)]
-    pad = jnp.zeros((3, 2 * rank - rank), f32)
-    box_rows = jnp.concatenate([skeleton_box[b] for b in range(boxes)], axis=1)
-    dev_rows = jnp.concatenate([skeleton_device[0], pad], axis=1)
-    row_list = [box_rows, dev_rows]
-    row_list += [jnp.concatenate([partner_top[h], pad], axis=1) for h in range(levels)]
-    all_rows = jnp.concatenate(row_list, axis=0)
-    all_rows = jnp.pad(all_rows, ((0, -all_rows.shape[0] % 16), (0, 0)))
-    columns_of = jnp.concatenate(
-        [skeleton_box.reshape(-1, rank), skeleton_device.reshape(-1, rank), own_top.reshape(-1, rank)], axis=0
-    ).T
-    columns_of = jnp.pad(columns_of, ((0, 0), (0, 128 - columns_of.shape[1])))
-
-    kinds = [pl.BlockSpec(memory_space=pltpu.SMEM)] * 3 + [pl.BlockSpec(memory_space=pltpu.VMEM)] * 15
+
+    kinds = [pl.BlockSpec(memory_space=pltpu.SMEM)] * 4 + [pl.BlockSpec(memory_space=pltpu.VMEM)] * 15
     dma = pltpu.SemaphoreType.DMA
     return pl.pallas_call(
-        functools.partial(kernel, G, L, slots, 8),
+        functools.partial(kernel, G, L, slots, slots),
         out_shape=jax.ShapeDtypeStruct(vectors.shape, f32),
         in_specs=kinds,
         out_specs=pl.BlockSpec(memory_space=pltpu.VMEM),
         scratch_shapes=[
+            pltpu.VMEM((16, 2 * rank), f32),
+            pltpu.VMEM((32, 2 * rank), f32),
+            pltpu.VMEM((leaves, 16, size), bf16),
             pltpu.VMEM((G * leaves + 1, columns + 16, size), bf16),
-            pltpu.VMEM((G * leaves + 1, size, 16), bf16),
             pltpu.VMEM((G, boxes + 2, columns, 2 * rank), bf16),
             pltpu.VMEM((G * L, columns + 48, 2 * rank), bf16),
             pltpu.VMEM((L, columns, 2 * rank), bf16),
@@ -349,8 +331,10 @@
             collective_id=0, has_side_effects=True, vmem_limit_bytes=56 * 1024 * 1024
         ),
     )(
-        near_ids, box_ids, dev_ids, vectors, source, target, basis_up, basis_down, up_leaf, down_leaf,
-        up_box, down_box, up_device, down_device, all_rows, columns_of, up_top, down_top,
+        near_list, near_count, far_box, far_device,
+        vectors, coords, basis_up, basis_down, up_leaf, down_leaf,
+        up_box, down_box, up_device, down_device,
+        skeleton_box, skeleton_device, skeleton_top, up_top, down_top,
     )
 
 

time: 88.6 us -> 64.5 us (0.73)
  Pallas kernels: 74.8 us -> 58.1 us
  local copies, waits for them, and re-layouts: 12.2 us -> 6.18 us
  other arithmetic: 1.02 us -> 0 us
    pallas_call x1, Pallas kernels: 74.8 us -> 58.1 us  [on_device(): pl.pallas_call(functools.partial(kernel, G, L, slots, slots), out_shape=j...]
    another operation x5 -> x0, local copies, waits for them, and re-layouts: 3.22 us -> none  [the longest x1 1.62 us: on_device(): target = jnp.stack(right, axis=1).astype(bf16)]
    reshape x4 -> x0, local copies, waits for them, and re-layouts: 1.29 us -> none  [the longest x1 0.66 us: on_device(): jnp.where(live, near_list - ml * (G * leaves), G * leaves).reshape(-1)]
    pad x2 -> x0, local copies, waits for them, and re-layouts: 1.21 us -> none  [the longest x1 0.61 us: on_device(): columns_of = jnp.pad(columns_of, ((0, 0), (0, 128 - columns_of.shape[1])))]
    gather x3 -> x0, local copies, waits for them, and re-layouts: 1.14 us -> none  [the longest x2 0.57 us: on_device(): own_top = skeleton_top[start + position]]
    unnamed x24 -> x9, local copies, waits for them, and re-layouts: 5.07 us -> 6.18 us
where the time goes in v2:
time: 64.5 us; the launch traced here: 64.3 us
  Pallas kernels  58.1 us (90%)
  local copies, waits for them, and re-layouts  6.18 us (10%)
    pallas_call x1, Pallas kernels, on_device(): pl.pallas_call(functools.partial(kernel, G, L, slots, slots), out_shape=j...  58.1 us
    unnamed x9, local copies, waits for them, and re-layouts  6.18 us

profile of v2, /device:TPU:1, one launch (start us, length us, event | category | flops | bytes accessed | tf_op | source)
XLA Modules:
  0.0 64.3 jit_solution(12634019589247232162)
XLA Ops:
  0.0 0.0 copy-start.1
  0.0 1.3 %copy.22.skeleton_device = f32[1,3,64]{2,1,0:T(4,128)} copy(f32[1,3,64]{2,0,1:T(1,128)} %param.31) | data formatting | bytes 1536 | tf_op args[12]
  1.3 0.0 copy-done.1
  1.3 0.6 copy.21.skeleton_box
  1.9 0.0 copy-start
  1.9 1.4 %copy.20.coords = bf16[16,3,256]{2,1,0:T(4,128)(2,1)} copy(bf16[16,3,256]{2,0,1:T(8,128)(2,1)} %param.19) | data formatting | bytes 49152 | tf_op args[0]
  3.3 0.0 copy-done
  3.3 0.6 copy.23.skeleton_top
  3.9 58.1 %shard_map.181 = f32[16,64,256]{2,1,0:T(8,128)} custom-call(s32[16,16]{1,0:T(8,128)} %near_list.1, s32[16]{0:T(128)} %near_count.1, s32[2,8]{1,0:T(2,128)} %far_box.1, s32[1,8]{1,0:T(1,128)} %far_device.1, f32[16,64,256]{2,1,0:T(8,128)} %vectors.1, bf16[16,3,256]{2,1,0:T(4,128)(2,1)} %copy.20.coords, f32[16,64,256]{2,1,0:T(8,128)} %basis_up.1, ...), custom_call_target="tpu_custom_call" | custom-call | tf_op jit(solution)/shard_map/pallas_call | solution.py:314
  62.0 2.3 %copy.25 = f32[16,64,256]{2,1,0:T(8,128)} copy(f32[16,64,256]{2,1,0:T(8,128)} %shard_map.181) | data formatting | bytes 2097152
Async XLA Ops:
  0.0 1.3 %copy-start.1 = (f32[2,3,64]{2,0,1:T(2,128)S(1)}, f32[2,3,64]{2,0,1:T(2,128)}, u32[]{:S(2)}) copy-start(f32[2,3,64]{2,0,1:T(2,128)} %param.27) | copy-start | bytes 4612
  1.9 1.4 %copy-start = (f32[16,3,64]{2,0,1:T(8,128)S(1)}, f32[16,3,64]{2,0,1:T(8,128)}, u32[]{:S(2)}) copy-start(f32[16,3,64]{2,0,1:T(8,128)} %param.35) | copy-start | bytes 36868

commit v3 on v2

--- a/solution.py
+++ b/solution.py
@@ -143,8 +143,8 @@
     dev_mine = me * L + ml
     dev_tab[dev_mine, :columns, :rank] = device[0]
     dev_tab[dev_mine, :columns, rank:] = device[1]
-    for p in range(3):
-        dev_tab[dev_mine, columns + 16 * p:columns + 16 * (p + 1)] = triples[p]
+    packed = [part.astype(f32)[3:6] for part in triples] + [jnp.zeros((7, 2 * rank), f32)]
+    dev_tab[dev_mine, columns:] = jnp.concatenate(packed, axis=0).astype(bf16)
     d_copies = []
     for k in range(1, L):
         spot = dev_tab.at[dev_mine]
@@ -196,9 +196,9 @@
     def own(first):
         return [cols[:, first + c:first + c + 1] for c in range(3)]
 
-    def joined(parts, first):
+    def joined(parts):
         whole = (parts[0].astype(f32) + parts[1].astype(f32)) + parts[2].astype(f32)
-        return whole[first:first + 3]
+        return whole[:3]
 
     box_down = []
     for b in range(boxes):
@@ -209,7 +209,7 @@
             w = jnp.bitwise_and(e, boxes - 1)
             payload = box_tab[n, w]
             skeleton = box_tab[n, boxes + 1]
-            whole = joined([skeleton[16 * p:16 * (p + 1)] for p in range(3)], 0)
+            whole = joined([skeleton[16 * p:16 * (p + 1)] for p in range(3)])
             whole = jnp.where(w == 0, whole[:, :rank], whole[:, rank:])
             matrix = coupling([whole[c:c + 1] for c in range(3)], own(3 * b))
             part = dot3((payload[:, :rank], payload[:, rank:]), matrix, NT)
@@ -250,7 +250,8 @@
         e = far_device[0, f]
         n = jnp.bitwise_and(e, G - 1)
         payload = dev_tab[n * L + jnp.bitwise_and(lax.shift_right_logical(e, G.bit_length() - 1), L - 1)]
-        whole = joined([payload[columns + 16 * p:columns + 16 * (p + 1)] for p in range(3)], 3)[:, :rank]
+        whole = payload[columns:].astype(f32)[:, :rank]
+        whole = (whole[:3] + whole[3:6]) + whole[6:9]
         matrix = coupling([whole[c:c + 1] for c in range(3)], own(3 * boxes))
         device_down += dot3((payload[:columns, :rank], payload[:columns, rank:]), matrix, NT)
     device_down = split(device_down)
@@ -322,7 +323,7 @@
             pltpu.VMEM((leaves, 16, size), bf16),
             pltpu.VMEM((G * leaves + 1, columns + 16, size), bf16),
             pltpu.VMEM((G, boxes + 2, columns, 2 * rank), bf16),
-            pltpu.VMEM((G * L, columns + 48, 2 * rank), bf16),
+            pltpu.VMEM((G * L, columns + 16, 2 * rank), bf16),
             pltpu.VMEM((L, columns, 2 * rank), bf16),
             dma((G,)), dma((G,)), dma((G,)), dma((G,)), dma((L,)), dma((L,)),
             dma((G,)), dma((G,)), dma((L,)), dma((L,)),

time: 64.5 us -> 63 us (0.977)
  Pallas kernels: 58.1 us -> 56.6 us
    pallas_call x1, Pallas kernels: 58.1 us -> 56.6 us  [on_device(): pl.pallas_call(functools.partial(kernel, G, L, slots, slots), out_shape=j...]
where the time goes in v3:
time: 63 us; the launch traced here: 62.8 us
  Pallas kernels  56.6 us (90%)
  local copies, waits for them, and re-layouts  6.18 us (10%)
    pallas_call x1, Pallas kernels, on_device(): pl.pallas_call(functools.partial(kernel, G, L, slots, slots), out_shape=j...  56.6 us
    unnamed x9, local copies, waits for them, and re-layouts  6.18 us

profile of v3, /device:TPU:1, one launch (start us, length us, event | category | flops | bytes accessed | tf_op | source)
XLA Modules:
  0.0 62.8 jit_solution(7554938361743382455)
XLA Ops:
  0.0 0.0 copy-start.1
  0.0 1.3 %copy.22.skeleton_device = f32[1,3,64]{2,1,0:T(4,128)} copy(f32[1,3,64]{2,0,1:T(1,128)} %param.31) | data formatting | bytes 1536 | tf_op args[12]
  1.3 0.0 copy-done.1
  1.3 0.6 copy.21.skeleton_box
  1.9 0.0 copy-start
  1.9 1.4 %copy.20.coords = bf16[16,3,256]{2,1,0:T(4,128)(2,1)} copy(bf16[16,3,256]{2,0,1:T(8,128)(2,1)} %param.19) | data formatting | bytes 49152 | tf_op args[0]
  3.3 0.0 copy-done
  3.3 0.6 copy.23.skeleton_top
  3.9 56.6 %shard_map.181 = f32[16,64,256]{2,1,0:T(8,128)} custom-call(s32[16,16]{1,0:T(8,128)} %near_list.1, s32[16]{0:T(128)} %near_count.1, s32[2,8]{1,0:T(2,128)} %far_box.1, s32[1,8]{1,0:T(1,128)} %far_device.1, f32[16,64,256]{2,1,0:T(8,128)} %vectors.1, bf16[16,3,256]{2,1,0:T(4,128)(2,1)} %copy.20.coords, f32[16,64,256]{2,1,0:T(8,128)} %basis_up.1, ...), custom_call_target="tpu_custom_call" | custom-call | tf_op jit(solution)/shard_map/pallas_call | solution.py:315
  60.5 2.3 %copy.25 = f32[16,64,256]{2,1,0:T(8,128)} copy(f32[16,64,256]{2,1,0:T(8,128)} %shard_map.181) | data formatting | bytes 2097152
Async XLA Ops:
  0.0 1.3 %copy-start.1 = (f32[2,3,64]{2,0,1:T(2,128)S(1)}, f32[2,3,64]{2,0,1:T(2,128)}, u32[]{:S(2)}) copy-start(f32[2,3,64]{2,0,1:T(2,128)} %param.27) | copy-start | bytes 4612
  1.9 1.4 %copy-start = (f32[16,3,64]{2,0,1:T(8,128)S(1)}, f32[16,3,64]{2,0,1:T(8,128)}, u32[]{:S(2)}) copy-start(f32[16,3,64]{2,0,1:T(8,128)} %param.35) | copy-start | bytes 36868
